TPU v7x, 32 devices: a whole 2x2x4 slice. The times are simulated.
32 devices in a mesh: groups: 2 (over y), gx: 4 (over z), gy: 2 (over x), gz: 2 (over core).
Axes of the slice: x: 2, y: 2, z: 4, core: 2. Of those that a mesh axis runs over, the one named last changes fastest.
Arguments:
- inputs: bfloat16 [1024, 6144], P(('groups', 'gx', 'gz'), 'gy'), parts along dimension 0, may hold values from -6 to 6
- cotangent: bfloat16 [1024, 6144], P(('groups', 'gx', 'gz'), 'gy'), parts along dimension 0, may hold values from -1.5 to 1.5
- up_weight: bfloat16 [49152, 6144], P(('gx', 'gz'), 'gy'), may hold values from -0.078125 to 0.078125
- down_weight: bfloat16 [49152, 6144], P(('gx', 'gz'), 'gy'), may hold values from -0.02734375 to 0.02734375
Outputs:
- outputs: bfloat16 [1024, 6144], P(('groups', 'gx', 'gz'), 'gy'), parts along dimension 0
- input_grad: bfloat16 [1024, 6144], P(('groups', 'gx', 'gz'), 'gy'), parts along dimension 0
There are 2 independent parts, one for each index of `groups`. A program takes and returns all parts, laid end to end along the dimension named above; an argument that names none is the same for every part. Nothing has to cross between parts.
All inputs are finite; a program needn't handle non-finite values.
Results may differ from a plain program's by a relative error of at most 0.018.
Values may be sent and summed in bfloat16 or wider, within the bound.
A program may use at most 256 MiB of HBM per device.

v0:
```python
import jax
import jax.numpy as jnp
from jax import lax
from jax.sharding import PartitionSpec as P

gelu_const = 0.7978845608028654


def gelu_value(value):
    inner = gelu_const * (value + 0.044715 * value * value * value)
    return 0.5 * value * (1.0 + jnp.tanh(inner))


def gelu_slope(value):
    inner = gelu_const * (value + 0.044715 * value * value * value)
    tanh_val = jnp.tanh(inner)
    return 0.5 * (1.0 + tanh_val) + 0.5 * value * (1.0 - tanh_val * tanh_val) * gelu_const * (
        1.0 + 3.0 * 0.044715 * value * value
    )


def inner_product(left, right):
    return lax.dot_general(
        left, right, (((1,), (1,)), ((), ())), preferred_element_type=jnp.float32
    )


def inner_term(left, right):
    return inner_product(left, right)


def outer_term(left, right):
    return jnp.dot(left, right, preferred_element_type=jnp.float32)


def body(inputs, cotangent, up_weight, down_weight):
    seen_inputs, seen_cotangent = (
        lax.all_gather(inputs, ("gx", "gz"), axis=0, tiled=True),
        lax.all_gather(cotangent, ("gx", "gz"), axis=0, tiled=True),
    )
    hidden_share = lax.psum_scatter(
        inner_term(seen_inputs, up_weight).astype(jnp.bfloat16),
        "gy",
        scatter_dimension=0,
        tiled=True,
    ).astype(jnp.float32)
    act_share = gelu_value(hidden_share).astype(jnp.bfloat16)
    act_rows = lax.all_gather(act_share, "gy", axis=0, tiled=True)
    outputs = lax.psum_scatter(
        outer_term(act_rows, down_weight).astype(jnp.bfloat16),
        ("gx", "gz"),
        scatter_dimension=0,
        tiled=True,
    )
    slope_share = lax.psum_scatter(
        inner_term(seen_cotangent, down_weight).astype(jnp.bfloat16),
        "gy",
        scatter_dimension=0,
        tiled=True,
    ).astype(jnp.float32)
    grad_share = (slope_share * gelu_slope(hidden_share)).astype(jnp.bfloat16)
    grad_rows = lax.all_gather(grad_share, "gy", axis=0, tiled=True)
    input_grad = lax.psum_scatter(
        outer_term(grad_rows, up_weight).astype(jnp.bfloat16),
        ("gx", "gz"),
        scatter_dimension=0,
        tiled=True,
    )
    return (outputs, input_grad)


def solution(mesh):
    placed = (
        P(("groups", "gx", "gz"), "gy"),
        P(("groups", "gx", "gz"), "gy"),
        P(("gx", "gz"), "gy"),
        P(("gx", "gz"), "gy"),
    )
    return jax.shard_map(
        body,
        mesh=mesh,
        in_specs=placed,
        out_specs=(P(("groups", "gx", "gz"), "gy"), P(("groups", "gx", "gz"), "gy")),
        check_vma=False,
    )
```

profile of v0, /device:TPU:0, one launch (start us, length us, event | category | flops | bytes accessed | tf_op | source)
XLA Modules:
  0.0 510.2 jit_solution(2757821665863851539)
XLA Ops:
  7.2 0.0 all-gather.9.cloned.1.call-start
  7.2 0.7 all-gather.9.cloned.1.call-update
  7.9 0.0 all-gather.5.cloned.1.call-start
  7.9 0.7 all-gather.5.cloned.1.call-update
  8.6 0.0 reduce-scatter.9.cloned.1.call-start
  8.7 42.0 %all-gather.9.cloned.1.call-done = bf16[512,3072]{1,0:T(8,128)(2,1)} async-done(((bf16[64,3072]{1,0:T(8,128)(2,1)}), bf16[512,3072]{1,0:T(8,128)(2,1)}) %all-gather.9.cloned.1.call-update) | async-done | bytes 3145744 | tf_op jit(solution)/shard_map/all_gather | solution.py:39
  50.7 26.9 %convolution_convert_fusion = bf16[512,6144]{1,0:T(8,128)(2,1)} fusion(bf16[512,3072]{1,0:T(8,128)(2,1)} %all-gather.9.cloned.1.call-done, bf16[6144,3072]{1,0:T(8,128)(2,1)} %param.7), kind=kOutput, calls=%fused_computation.7 | convolution fusion | flops 19330498560 | bytes 47185920 | tf_op jit(solution)/shard_map/dot_general | solution.py:23
  77.5 0.0 reduce-scatter.9.cloned.1.call-update
  77.6 0.0 reduce-scatter.5.cloned.1.call-start
  77.6 11.9 %all-gather.5.cloned.1.call-done = bf16[512,3072]{1,0:T(8,128)(2,1)} async-done(((bf16[64,3072]{1,0:T(8,128)(2,1)}), bf16[512,3072]{1,0:T(8,128)(2,1)}) %all-gather.5.cloned.1.call-update) | async-done | bytes 3145744 | tf_op jit(solution)/shard_map/all_gather | solution.py:38
  89.5 26.8 %convolution_convert_fusion.1 = bf16[512,6144]{1,0:T(8,128)(2,1)} fusion(bf16[512,3072]{1,0:T(8,128)(2,1)} %all-gather.5.cloned.1.call-done, bf16[6144,3072]{1,0:T(8,128)(2,1)} %param.6), kind=kOutput, calls=%fused_computation.8 | convolution fusion | flops 19330498560 | bytes 47185920 | tf_op jit(solution)/shard_map/dot_general | solution.py:23
  116.3 0.0 reduce-scatter.5.cloned.1.call-update
  116.3 0.2 all-gather.11.cloned.1.call-start
  116.6 51.1 %reduce-scatter.9.cloned.1.call-done = bf16[256,6144]{1,0:T(8,128)(2,1)} async-done(((bf16[512,6144]{1,0:T(8,128)(2,1)}), bf16[256,6144]{1,0:T(8,128)(2,1)}) %reduce-scatter.9.cloned.1.call-update) | async-done | bytes 3145744 | tf_op jit(solution)/shard_map/reduce_scatter | solution.py:55
  167.7 79.4 %reduce-scatter.5.cloned.1.call-done = bf16[256,6144]{1,0:T(8,128)(2,1)} async-done(((bf16[512,6144]{1,0:T(8,128)(2,1)}), bf16[256,6144]{1,0:T(8,128)(2,1)}) %reduce-scatter.5.cloned.1.call-update) | async-done | bytes 3145744 | tf_op jit(solution)/shard_map/reduce_scatter | solution.py:41
  247.1 8.3 %fusion.7 = (bf16[256,6144]{1,0:T(8,128)(2,1)}, bf16[256,6144]{1,0:T(8,128)(2,1)}) fusion(bf16[256,6144]{1,0:T(8,128)(2,1)} %reduce-scatter.5.cloned.1.call-done, bf16[256,6144]{1,0:T(8,128)(2,1)} %reduce-scatter.9.cloned.1.call-done), kind=kLoop, calls=%fused_computation.16 | loop fusion | flops 36175872 | bytes 12582912 | tf_op jit(solution)/shard_map/convert_element_type | solution.py:61
  255.3 0.0 all-gather.11.cloned.1.call-update
  255.4 0.0 all-gather.7.cloned.1.call-start
  255.4 0.5 all-gather.7.cloned.1.call-update
  256.0 0.0 reduce-scatter.11.cloned.1.call-start
  256.0 79.9 %all-gather.11.cloned.1.call-done = bf16[512,6144]{1,0:T(8,128)(2,1)} async-done(((bf16[256,6144]{1,0:T(8,128)(2,1)}), bf16[512,6144]{1,0:T(8,128)(2,1)}) %all-gather.11.cloned.1.call-update) | async-done | bytes 6291472 | tf_op jit(solution)/shard_map/all_gather | solution.py:62
  335.9 27.4 %convolution_convert_fusion.2 = bf16[512,3072]{1,0:T(8,128)(2,1)} fusion(bf16[512,6144]{1,0:T(8,128)(2,1)} %all-gather.11.cloned.1.call-done, bf16[6144,3072]{1,0:T(8,128)(2,1)} %param.6), kind=kOutput, calls=%fused_computation.20 | convolution fusion | flops 19328925696 | bytes 47185920 | tf_op jit(solution)/shard_map/dot_general | solution.py:33
  363.3 0.0 reduce-scatter.11.cloned.1.call-update
  363.4 0.0 reduce-scatter.7.cloned.1.call-start
  363.4 54.3 %all-gather.7.cloned.1.call-done = bf16[512,6144]{1,0:T(8,128)(2,1)} async-done(((bf16[256,6144]{1,0:T(8,128)(2,1)}), bf16[512,6144]{1,0:T(8,128)(2,1)}) %all-gather.7.cloned.1.call-update) | async-done | bytes 6291472 | tf_op jit(solution)/shard_map/all_gather | solution.py:48
  417.7 27.7 %convolution_convert_fusion.3 = bf16[512,3072]{1,0:T(8,128)(2,1)} fusion(bf16[512,6144]{1,0:T(8,128)(2,1)} %all-gather.7.cloned.1.call-done, bf16[6144,3072]{1,0:T(8,128)(2,1)} %param.7), kind=kOutput, calls=%fused_computation.21 | convolution fusion | flops 19328925696 | bytes 47185920 | tf_op jit(solution)/shard_map/dot_general | solution.py:33
  445.4 0.0 reduce-scatter.7.cloned.1.call-update
  445.4 15.6 %reduce-scatter.11.cloned.1.call-done = bf16[64,3072]{1,0:T(8,128)(2,1)} async-done(((bf16[512,3072]{1,0:T(8,128)(2,1)}), bf16[64,3072]{1,0:T(8,128)(2,1)}) %reduce-scatter.11.cloned.1.call-update) | async-done | bytes 393232 | tf_op jit(solution)/shard_map/reduce_scatter | solution.py:63
  461.0 42.4 %reduce-scatter.7.cloned.1.call-done = bf16[64,3072]{1,0:T(8,128)(2,1)} async-done(((bf16[512,3072]{1,0:T(8,128)(2,1)}), bf16[64,3072]{1,0:T(8,128)(2,1)}) %reduce-scatter.7.cloned.1.call-update) | async-done | bytes 393232 | tf_op jit(solution)/shard_map/reduce_scatter | solution.py:49
Async XLA Ops:
  7.2 43.5 %all-gather.9.cloned.1.call-start = ((), (), s32[]{:S(2)}) async-start(), calls=%async_computation.8 | async-start | bytes 3538944 | tf_op jit(solution)/shard_map/all_gather | solution.py:39
  7.9 81.6 %all-gather.5.cloned.1.call-start = ((), (), s32[]{:S(2)}) async-start(), calls=%async_computation.4 | async-start | bytes 3538944 | tf_op jit(solution)/shard_map/all_gather | solution.py:38
  8.6 159.1 %reduce-scatter.9.cloned.1.call-start = ((), (), s32[]{:S(2)}) async-start(), calls=%async_computation.9 | async-start | bytes 9437184 | tf_op jit(solution)/shard_map/reduce_scatter | solution.py:55
  77.6 169.5 %reduce-scatter.5.cloned.1.call-start = ((), (), s32[]{:S(2)}) async-start(), calls=%async_computation.5 | async-start | bytes 9437184 | tf_op jit(solution)/shard_map/reduce_scatter | solution.py:41
  116.3 219.6 %all-gather.11.cloned.1.call-start = ((), (), s32[]{:S(2)}) async-start(), calls=%async_computation.10 | async-start | bytes 9437184 | tf_op jit(solution)/shard_map/all_gather | solution.py:62
  255.4 162.3 %all-gather.7.cloned.1.call-start = ((), (), s32[]{:S(2)}) async-start(), calls=%async_computation.6 | async-start | bytes 9437184 | tf_op jit(solution)/shard_map/all_gather | solution.py:48
  256.0 205.0 %reduce-scatter.11.cloned.1.call-start = ((), (), s32[]{:S(2)}) async-start(), calls=%async_computation.11 | async-start | bytes 3538944 | tf_op jit(solution)/shard_map/reduce_scatter | solution.py:63
  363.4 140.0 %reduce-scatter.7.cloned.1.call-start = ((), (), s32[]{:S(2)}) async-start(), calls=%async_computation.7 | async-start | bytes 3538944 | tf_op jit(solution)/shard_map/reduce_scatter | solution.py:49
Sparse Core Ops, SparseCore 0:
  9.6 40.9 all-gather.8
  52.3 37.1 all-gather.4
  91.8 75.8 reduce-scatter.8
  170.0 77.0 reduce-scatter.4
  255.5 80.3 all-gather.10
  337.3 80.3 all-gather.6
  420.6 40.3 reduce-scatter.10
  463.8 39.4 reduce-scatter.6
where the time goes:
time: 510 us
  waiting for transfers between devices  378 us (74%)
  matrix products  109 us (21%)
  between operations  14.1 us (3%)
  other arithmetic  8.26 us (2%)
    all_gather x1, waiting for transfers between devices, body(): grad_rows = lax.all_gather(grad_share, 'gy', axis=0, tiled=True)  79.9 us
    reduce_scatter x1, waiting for transfers between devices, body(): lax.psum_scatter(inner_term(seen_inputs, up_weight).astype(jnp.bfloat16),...  79.4 us
    dot_general x2, matrix products, outer_term(): return jnp.dot(left, right, preferred_element_type=jnp.float32)  55.1 us
    all_gather x1, waiting for transfers between devices, body(): act_rows = lax.all_gather(act_share, 'gy', axis=0, tiled=True)  54.3 us
    dot_general x2, matrix products, inner_product(): lax.dot_general(left, right, (((1,), (1,)), ((), ())), preferred_element_...  53.7 us
    reduce_scatter x1, waiting for transfers between devices, body(): lax.psum_scatter(inner_term(seen_cotangent, down_weight).astype(jnp.bfloa...  51.1 us
    reduce_scatter x1, waiting for transfers between devices, body(): lax.psum_scatter(outer_term(act_rows, down_weight).astype(jnp.bfloat16),...  42.4 us
    all_gather x1, waiting for transfers between devices, body(): lax.all_gather(cotangent, ('gx', 'gz'), axis=0, tiled=True)  42 us
  transfers between devices with their start and end apart: 8, of which 8 were waited for; matrix products, arithmetic and copies ran while one was open for 21% of the time, Pallas kernels for 0%

commit v1 on v0

--- a/solution.py
+++ b/solution.py
@@ -69,6 +69,66 @@
     return (outputs, input_grad)
 
 
+def ordered(value, earlier):
+    return lax.optimization_barrier((value, earlier))[0]
+
+
+def pair_body(pieces, inputs, cotangent, up_weight, down_weight):
+    width = up_weight.shape[0] // pieces
+    sent = []
+
+    def swap(term):
+        if len(sent) >= 2:
+            term = ordered(term, sent[-2])
+        other = lax.ppermute(term, "gy", [(0, 1), (1, 0)])
+        sent.append(other)
+        return other
+
+    def gather(rows):
+        return lax.all_gather(rows, ("gx", "gz"), axis=0, tiled=True)
+
+    def scatter(total):
+        return lax.psum_scatter(
+            total.astype(jnp.bfloat16), ("gx", "gz"), scatter_dimension=0, tiled=True
+        )
+
+    def part(weight, piece):
+        return weight[piece * width : (piece + 1) * width]
+
+    seen_inputs = gather(inputs)
+    seen_cotangent = gather(ordered(cotangent, inputs))
+    hidden = []
+    for piece in range(pieces):
+        term = inner_term(seen_inputs, part(up_weight, piece)).astype(jnp.bfloat16)
+        hidden.append((term, swap(term)))
+    slope = []
+    for piece in range(pieces):
+        term = inner_term(seen_cotangent, part(down_weight, piece)).astype(jnp.bfloat16)
+        slope.append((term, swap(term)))
+    values = [a.astype(jnp.float32) + b.astype(jnp.float32) for a, b in hidden]
+    out_total = 0.0
+    for piece in range(pieces):
+        act = gelu_value(values[piece]).astype(jnp.bfloat16)
+        out_total += outer_term(act, part(down_weight, piece))
+    outputs = scatter(out_total)
+    grad_total = 0.0
+    for piece in range(pieces):
+        a, b = slope[piece]
+        total = a.astype(jnp.float32) + b.astype(jnp.float32)
+        grad = (total * gelu_slope(values[piece])).astype(jnp.bfloat16)
+        grad_total += outer_term(grad, part(up_weight, piece))
+    return (outputs, scatter(grad_total))
+
+
+def chosen_body(mesh):
+    def run(inputs, cotangent, up_weight, down_weight):
+        if mesh.shape["gy"] != 2 or up_weight.shape[0] % 1024 != 0:
+            return body(inputs, cotangent, up_weight, down_weight)
+        return pair_body(4, inputs, cotangent, up_weight, down_weight)
+
+    return run
+
+
 def solution(mesh):
     placed = (
         P(("groups", "gx", "gz"), "gy"),
@@ -77,7 +137,7 @@
         P(("gx", "gz"), "gy"),
     )
     return jax.shard_map(
-        body,
+        chosen_body(mesh),
         mesh=mesh,
         in_specs=placed,
         out_specs=(P(("groups", "gx", "gz"), "gy"), P(("groups", "gx", "gz"), "gy")),

time: 510 us -> 409 us (0.80); the launches traced: 510 us -> 402 us
  waiting for transfers between devices: 378 us -> 181 us
  matrix products: 109 us -> 197 us
  starting transfers between devices: 0.5 us -> 9.86 us
  other arithmetic: 8.26 us -> 0 us
    reduce_scatter x4 -> x2, waiting for transfers between devices: 188 us -> 39.3 us  [scatter(): lax.psum_scatter(total.astype(jnp.bfloat16), ('gx', 'gz'), scatter_dimens...]
    all_gather x4 -> x2, waiting for transfers between devices: 188 us -> 43.2 us  [gather(): return lax.all_gather(rows, ('gx', 'gz'), axis=0, tiled=True)]
    ppermute x0 -> x8, waiting for transfers between devices: none -> 97 us  [swap(): other = lax.ppermute(term, 'gy', [(0, 1), (1, 0)])]
    dot_general x2 -> x8, matrix products: 55.1 us -> 112 us  [outer_term(): return jnp.dot(left, right, preferred_element_type=jnp.float32)]
    dot_general x2 -> x8, matrix products: 53.7 us -> 84.9 us  [inner_product(): lax.dot_general(left, right, (((1,), (1,)), ((), ())), preferred_element_...]
    ppermute x0 -> x8, starting transfers between devices: none -> 9.3 us  [swap(): other = lax.ppermute(term, 'gy', [(0, 1), (1, 0)])]
    convert_element_type x1 -> x0, other arithmetic: 8.26 us -> none  [body(): grad_share = (slope_share * gelu_slope(hidden_share)).astype(jnp.bfloat16)]
  transfers between devices with their start and end apart: 8 -> 12, of which waited for: 8 -> 7; matrix products, arithmetic and copies ran while one was open for 21% -> 49% of each run, Pallas kernels for 0% -> 0%
where the time goes in v1:
time: 409 us; the launch traced here: 402 us
  matrix products  197 us (48%)
  waiting for transfers between devices  181 us (44%)
  between operations  14 us (3%)
  starting transfers between devices  9.86 us (2%)
    dot_general x8, matrix products, outer_term(): return jnp.dot(left, right, preferred_element_type=jnp.float32)  112 us
    ppermute x8, waiting for transfers between devices, swap(): other = lax.ppermute(term, 'gy', [(0, 1), (1, 0)])  97 us
    dot_general x8, matrix products, inner_product(): lax.dot_general(left, right, (((1,), (1,)), ((), ())), preferred_element_...  84.9 us
    all_gather x2, waiting for transfers between devices, gather(): return lax.all_gather(rows, ('gx', 'gz'), axis=0, tiled=True)  43.2 us
    reduce_scatter x2, waiting for transfers between devices, scatter(): lax.psum_scatter(total.astype(jnp.bfloat16), ('gx', 'gz'), scatter_dimens...  39.3 us
    ppermute x8, starting transfers between devices, swap(): other = lax.ppermute(term, 'gy', [(0, 1), (1, 0)])  9.3 us
  transfers between devices with their start and end apart: 12, of which 7 were waited for; matrix products, arithmetic and copies ran while one was open for 49% of the time, Pallas kernels for 0%

profile of v1, /device:TPU:0, one launch (start us, length us, event | category | flops | bytes accessed | tf_op | source)
XLA Modules:
  0.0 402.2 jit_solution(2457263350524318130)
XLA Ops:
  7.2 0.0 all-gather.3.cloned.1.call-start
  7.2 0.7 all-gather.3.cloned.1.call-update
  7.9 0.0 all-gather.5.cloned.1.call-start
  7.9 0.7 all-gather.5.cloned.1.call-update
  8.6 0.0 reduce-scatter.3.cloned.1.call-start
  8.7 42.0 %all-gather.3.cloned.1.call-done = bf16[512,3072]{1,0:T(8,128)(2,1)} async-done(((bf16[64,3072]{1,0:T(8,128)(2,1)}), bf16[512,3072]{1,0:T(8,128)(2,1)}) %all-gather.3.cloned.1.call-update) | async-done | bytes 3145744 | tf_op jit(solution)/shard_map/all_gather | solution.py:88
  50.7 0.0 copy-start.1
  50.7 9.6 %fusion.70 = bf16[512,1536]{1,0:T(8,128)(2,1)S(1)} fusion(bf16[512,3072]{1,0:T(8,128)(2,1)} %all-gather.3.cloned.1.call-done, bf16[6144,3072]{1,0:T(8,128)(2,1)} %param.6), kind=kOutput, calls=%fused_computation.80 | convolution fusion | flops 4832624640 | bytes 14155776 | tf_op jit(solution)/shard_map/dot_general | solution.py:23
  60.3 1.5 collective-permute-start.1
  61.8 0.0 copy-done.1
  61.8 8.9 %fusion.64 = bf16[512,1536]{1,0:T(8,128)(2,1)} fusion(bf16[512,3072]{1,0:T(8,128)(2,1)S(1)} %copy-done.1, bf16[6144,3072]{1,0:T(8,128)(2,1)} %param.6), kind=kOutput, calls=%fused_computation.78 | convolution fusion | flops 4832624640 | bytes 14155776 | tf_op jit(solution)/shard_map/dot_general | solution.py:23
  70.7 0.6 collective-permute-start
  71.3 7.9 %fusion.82 = bf16[512,1536]{1,0:T(8,128)(2,1)S(1)} fusion(bf16[512,3072]{1,0:T(8,128)(2,1)S(1)} %copy-done.1, bf16[6144,3072]{1,0:T(8,128)(2,1)} %param.6), kind=kOutput, calls=%fused_computation.84 | convolution fusion | flops 4832624640 | bytes 14155776 | tf_op jit(solution)/shard_map/dot_general | solution.py:23
  79.2 9.1 %fusion.76 = bf16[512,1536]{1,0:T(8,128)(2,1)} fusion(bf16[512,3072]{1,0:T(8,128)(2,1)S(1)} %copy-done.1, bf16[6144,3072]{1,0:T(8,128)(2,1)} %param.6), kind=kOutput, calls=%fused_computation.82 | convolution fusion | flops 4832624640 | bytes 14155776 | tf_op jit(solution)/shard_map/dot_general | solution.py:23
  88.2 1.2 all-gather.5.cloned.1.call-done
  89.5 0.0 copy-start
  89.5 10.5 %fusion.79 = bf16[512,1536]{1,0:T(8,128)(2,1)} fusion(bf16[512,3072]{1,0:T(8,128)(2,1)} %all-gather.5.cloned.1.call-done, bf16[6144,3072]{1,0:T(8,128)(2,1)} %param.7), kind=kOutput, calls=%fused_computation.83 | convolution fusion | flops 4832624640 | bytes 14155776 | tf_op jit(solution)/shard_map/dot_general | solution.py:23
  100.0 0.0 copy-done
  100.0 20.9 %fusion.67 = bf16[512,1536]{1,0:T(8,128)(2,1)} fusion(bf16[512,3072]{1,0:T(8,128)(2,1)S(1)} %copy-done, bf16[6144,3072]{1,0:T(8,128)(2,1)} %param.7), kind=kOutput, calls=%fused_computation.79 | convolution fusion | flops 4832624640 | bytes 14155776 | tf_op jit(solution)/shard_map/dot_general | solution.py:23
  120.9 0.0 copy-start.2
  120.9 9.1 %fusion.73 = bf16[512,1536]{1,0:T(8,128)(2,1)} fusion(bf16[512,3072]{1,0:T(8,128)(2,1)S(1)} %copy-done, bf16[6144,3072]{1,0:T(8,128)(2,1)} %param.7), kind=kOutput, calls=%fused_computation.81 | convolution fusion | flops 4832624640 | bytes 14155776 | tf_op jit(solution)/shard_map/dot_general | solution.py:23
  129.9 0.0 collective-permute-done.1
  129.9 1.5 collective-permute-start.3
  131.4 0.0 collective-permute-done
  131.4 0.0 copy-done.2
  131.4 0.7 collective-permute-start.2
  132.1 9.0 %fusion.85 = bf16[512,1536]{1,0:T(8,128)(2,1)} fusion(bf16[512,3072]{1,0:T(8,128)(2,1)S(1)} %copy-done, bf16[6144,3072]{1,0:T(8,128)(2,1)} %param.7), kind=kOutput, calls=%fused_computation.85 | convolution fusion | flops 4832624640 | bytes 14155776 | tf_op jit(solution)/shard_map/dot_general | solution.py:23
  141.1 10.7 %fusion.18 = f32[512,3072]{1,0:T(8,128)} fusion(bf16[6144,3072]{1,0:T(8,128)(2,1)} %param.7, bf16[512,1536]{1,0:T(8,128)(2,1)} %collective-permute-done.1, bf16[512,1536]{1,0:T(8,128)(2,1)S(1)} %fusion.70), kind=kOutput, calls=%fused_computation.18 | convolution fusion | flops 4841275392 | bytes 18874368 | tf_op jit(solution)/shard_map/dot_general | solution.py:33
  151.8 48.4 %collective-permute-done.2 = bf16[512,1536]{1,0:T(8,128)(2,1)S(1)} collective-permute-done((bf16[512,1536]{1,0:T(8,128)(2,1)S(1)}, bf16[512,1536]{1,0:T(8,128)(2,1)S(1)}, u32[]{:S(2)}, u32[]{:S(2)}) %collective-permute-start.2) | collective-permute-done | bytes 1572896 | tf_op jit(solution)/shard_map/ppermute | solution.py:83
  200.2 0.0 copy-start.7
  200.2 1.5 collective-permute-start.4
  201.6 0.0 collective-permute-done.3
  201.6 0.0 copy-start.5
  201.6 0.6 collective-permute-start.5
  202.2 11.1 %fusion.2 = f32[512,3072]{1,0:T(8,128)} fusion(bf16[6144,3072]{1,0:T(8,128)(2,1)} %param.7, bf16[512,1536]{1,0:T(8,128)(2,1)S(1)} %collective-permute-done.3, bf16[512,1536]{1,0:T(8,128)(2,1)S(1)} %fusion.82), kind=kOutput, calls=%fused_computation.2 | convolution fusion | flops 4841275392 | bytes 18874368 | tf_op jit(solution)/shard_map/dot_general | solution.py:33
  213.4 0.0 copy-done.7
  213.4 0.0 copy-done.5
  213.4 11.2 %fusion.10 = f32[512,3072]{1,0:T(8,128)} fusion(bf16[6144,3072]{1,0:T(8,128)(2,1)} %param.7, bf16[512,1536]{1,0:T(8,128)(2,1)S(1)} %collective-permute-done.2, bf16[512,1536]{1,0:T(8,128)(2,1)S(1)} %copy-done.2), kind=kOutput, calls=%fused_computation.10 | convolution fusion | flops 4841275392 | bytes 18874368 | tf_op jit(solution)/shard_map/dot_general | solution.py:33
  224.5 17.4 %add_convert_fusion.1 = bf16[512,3072]{1,0:T(8,128)(2,1)} fusion(f32[512,3072]{1,0:T(8,128)} %fusion.2, f32[512,3072]{1,0:T(8,128)} %fusion.10, f32[512,3072]{1,0:T(8,128)} %fusion.18, bf16[6144,3072]{1,0:T(8,128)(2,1)} %param.7, bf16[512,1536]{1,0:T(8,128)(2,1)} %collective-permute-done, bf16[512,1536]{1,0:T(8,128)(2,1)} %fusion.64), kind=kOutput, calls=%fused_computation.33 | convolution fusion | flops 4847566848 | bytes 34603008 | tf_op jit(solution)/shard_map/dot_general | solution.py:33
  242.0 0.0 reduce-scatter.3.cloned.1.call-update
  242.0 0.4 reduce-scatter.5.cloned.1.call-start
  242.4 0.0 collective-permute-done.4
  242.5 1.5 collective-permute-start.6
  244.0 27.5 %collective-permute-done.5 = bf16[512,1536]{1,0:T(8,128)(2,1)} collective-permute-done((bf16[512,1536]{1,0:T(8,128)(2,1)}, bf16[512,1536]{1,0:T(8,128)(2,1)}, u32[]{:S(2)}, u32[]{:S(2)}) %collective-permute-start.5) | collective-permute-done | bytes 1572896 | tf_op jit(solution)/shard_map/ppermute | solution.py:83
  271.5 1.5 collective-permute-start.7
  273.0 15.2 %fusion.28 = f32[512,3072]{1,0:T(8,128)} fusion(bf16[6144,3072]{1,0:T(8,128)(2,1)} %param.6, bf16[512,1536]{1,0:T(8,128)(2,1)} %collective-permute-done.4, bf16[512,1536]{1,0:T(8,128)(2,1)} %fusion.67, bf16[512,1536]{1,0:T(8,128)(2,1)} %collective-permute-done, bf16[512,1536]{1,0:T(8,128)(2,1)} %fusion.64), kind=kOutput, calls=%fused_computation.28 | convolution fusion | flops 4851499008 | bytes 22020096 | tf_op jit(solution)/shard_map/dot_general | solution.py:33
  288.2 0.0 copy-start.3
  288.2 0.0 copy-start.4
  288.2 0.0 copy-start.8
  288.2 14.7 %fusion.20 = f32[512,3072]{1,0:T(8,128)} fusion(bf16[6144,3072]{1,0:T(8,128)(2,1)} %param.6, bf16[512,1536]{1,0:T(8,128)(2,1)} %collective-permute-done.5, bf16[512,1536]{1,0:T(8,128)(2,1)} %fusion.73, bf16[512,1536]{1,0:T(8,128)(2,1)} %collective-permute-done.1, bf16[512,1536]{1,0:T(8,128)(2,1)S(1)} %fusion.70), kind=kOutput, calls=%fused_computation.20 | convolution fusion | flops 4851499008 | bytes 22020096 | tf_op jit(solution)/shard_map/dot_general | solution.py:33
  302.9 0.0 copy-start.6
  302.9 2.2 collective-permute-done.6
  305.1 0.0 copy-done.3
  305.1 0.0 copy-done.4
  305.1 0.0 copy-done.8
  305.1 13.3 %fusion.12 = f32[512,3072]{1,0:T(8,128)} fusion(bf16[6144,3072]{1,0:T(8,128)(2,1)} %param.6, bf16[512,1536]{1,0:T(8,128)(2,1)S(1)} %collective-permute-done.6, bf16[512,1536]{1,0:T(8,128)(2,1)S(1)} %copy-done.4, bf16[512,1536]{1,0:T(8,128)(2,1)S(1)} %copy-done.8, bf16[512,1536]{1,0:T(8,128)(2,1)S(1)} %copy-done.3), kind=kOutput, calls=%fused_computation.12 | convolution fusion | flops 4851499008 | bytes 22020096 | tf_op jit(solution)/shard_map/dot_general | solution.py:33
  318.4 18.9 %collective-permute-done.7 = bf16[512,1536]{1,0:T(8,128)(2,1)} collective-permute-done((bf16[512,1536]{1,0:T(8,128)(2,1)}, bf16[512,1536]{1,0:T(8,128)(2,1)}, u32[]{:S(2)}, u32[]{:S(2)}) %collective-permute-start.7) | collective-permute-done | bytes 1572896 | tf_op jit(solution)/shard_map/ppermute | solution.py:83
  337.3 0.0 copy-done.6
  337.3 18.8 %add_convert_fusion = bf16[512,3072]{1,0:T(8,128)(2,1)} fusion(f32[512,3072]{1,0:T(8,128)} %fusion.12, f32[512,3072]{1,0:T(8,128)} %fusion.28, f32[512,3072]{1,0:T(8,128)} %fusion.20, bf16[6144,3072]{1,0:T(8,128)(2,1)} %param.6, bf16[512,1536]{1,0:T(8,128)(2,1)} %collective-permute-done.7, bf16[512,1536]{1,0:T(8,128)(2,1)} %fusion.85, ...), kind=kOutput, calls=%fused_computation.32 | convolution fusion | flops 4857790464 | bytes 37748736 | tf_op jit(solution)/shard_map/dot_general | solution.py:33
  356.1 0.0 reduce-scatter.5.cloned.1.call-update
  356.1 0.0 reduce-scatter.3.cloned.1.call-done
  356.2 39.3 %reduce-scatter.5.cloned.1.call-done = bf16[64,3072]{1,0:T(8,128)(2,1)} async-done(((bf16[512,3072]{1,0:T(8,128)(2,1)}), bf16[64,3072]{1,0:T(8,128)(2,1)}) %reduce-scatter.5.cloned.1.call-update) | async-done | bytes 393232 | tf_op jit(solution)/shard_map/reduce_scatter | solution.py:91
Async XLA Ops:
  7.2 43.5 %all-gather.3.cloned.1.call-start = ((), (), s32[]{:S(2)}) async-start(), calls=%async_computation.2 | async-start | bytes 3538944 | tf_op jit(solution)/shard_map/all_gather | solution.py:88
  7.9 81.6 %all-gather.5.cloned.1.call-start = ((), (), s32[]{:S(2)}) async-start(), calls=%async_computation.4 | async-start | bytes 3538944 | tf_op jit(solution)/shard_map/all_gather | solution.py:88
  8.6 347.5 %reduce-scatter.3.cloned.1.call-start = ((), (), s32[]{:S(2)}) async-start(), calls=%async_computation.3 | async-start | bytes 3538944 | tf_op jit(solution)/shard_map/reduce_scatter | solution.py:91
  50.7 11.1 %copy-start.1 = (bf16[512,3072]{1,0:T(8,128)(2,1)S(1)}, bf16[512,3072]{1,0:T(8,128)(2,1)}, u32[]{:S(2)}) copy-start(bf16[512,3072]{1,0:T(8,128)(2,1)} %all-gather.3.cloned.1.call-done) | copy-start | bytes 9437188
  60.3 69.7 %collective-permute-start.1 = (bf16[512,1536]{1,0:T(8,128)(2,1)S(1)}, bf16[512,1536]{1,0:T(8,128)(2,1)}, u32[]{:S(2)}, u32[]{:S(2)}) collective-permute-start(bf16[512,1536]{1,0:T(8,128)(2,1)S(1)} %fusion.70), channel_id=1, source_target_pairs={{0,2},{2,0},{1,3},{3,1},{4,6},{6,4},{5,7},{7,5},{8,10},{10,8},{9,1... | collective-permute-start | bytes 4718600 | tf_op jit(solution)/shard_map/ppermute | solution.py:83
  70.7 60.7 %collective-permute-start = (bf16[512,1536]{1,0:T(8,128)(2,1)}, bf16[512,1536]{1,0:T(8,128)(2,1)}, u32[]{:S(2)}, u32[]{:S(2)}) collective-permute-start(bf16[512,1536]{1,0:T(8,128)(2,1)} %fusion.64), channel_id=1, source_target_pairs={{0,2},{2,0},{1,3},{3,1},{4,6},{6,4},{5,7},{7,5},{8,10},{10,8},{9,1... | collective-permute-start | bytes 4718600 | tf_op jit(solution)/shard_map/ppermute | solution.py:83
  89.5 10.5 %copy-start = (bf16[512,3072]{1,0:T(8,128)(2,1)S(1)}, bf16[512,3072]{1,0:T(8,128)(2,1)}, u32[]{:S(2)}) copy-start(bf16[512,3072]{1,0:T(8,128)(2,1)} %all-gather.5.cloned.1.call-done) | copy-start | bytes 9437188
  120.9 10.5 %copy-start.2 = (bf16[512,1536]{1,0:T(8,128)(2,1)S(1)}, bf16[512,1536]{1,0:T(8,128)(2,1)}, u32[]{:S(2)}) copy-start(bf16[512,1536]{1,0:T(8,128)(2,1)} %fusion.76) | copy-start | bytes 4718596
  129.9 71.7 %collective-permute-start.3 = (bf16[512,1536]{1,0:T(8,128)(2,1)S(1)}, bf16[512,1536]{1,0:T(8,128)(2,1)S(1)}, u32[]{:S(2)}, u32[]{:S(2)}) collective-permute-start(bf16[512,1536]{1,0:T(8,128)(2,1)S(1)} %fusion.82), channel_id=1, source_target_pairs={{0,2},{2,0},{1,3},{3,1},{4,6},{6,4},{5,7},{7,5},{8,10},{10,8},{9,1... | collective-permute-start | bytes 4718600 | tf_op jit(solution)/shard_map/ppermute | solution.py:83
  131.4 68.8 %collective-permute-start.2 = (bf16[512,1536]{1,0:T(8,128)(2,1)S(1)}, bf16[512,1536]{1,0:T(8,128)(2,1)S(1)}, u32[]{:S(2)}, u32[]{:S(2)}) collective-permute-start(bf16[512,1536]{1,0:T(8,128)(2,1)S(1)} %copy-done.2), channel_id=1, source_target_pairs={{0,2},{2,0},{1,3},{3,1},{4,6},{6,4},{5,7},{7,5},{8,10},{10,8},{9,1... | collective-permute-start | bytes 4718600 | tf_op jit(solution)/shard_map/ppermute | solution.py:83
  200.2 13.2 %copy-start.7 = (bf16[512,1536]{1,0:T(8,128)(2,1)}, bf16[512,1536]{1,0:T(8,128)(2,1)S(1)}, u32[]{:S(2)}) copy-start(bf16[512,1536]{1,0:T(8,128)(2,1)S(1)} %collective-permute-done.2) | copy-start | bytes 4718596
  200.2 42.3 %collective-permute-start.4 = (bf16[512,1536]{1,0:T(8,128)(2,1)}, bf16[512,1536]{1,0:T(8,128)(2,1)}, u32[]{:S(2)}, u32[]{:S(2)}) collective-permute-start(bf16[512,1536]{1,0:T(8,128)(2,1)} %fusion.67), channel_id=1, source_target_pairs={{0,2},{2,0},{1,3},{3,1},{4,6},{6,4},{5,7},{7,5},{8,10},{10,8},{9,1... | collective-permute-start | bytes 4718600 | tf_op jit(solution)/shard_map/ppermute | solution.py:83
  201.6 11.7 %copy-start.5 = (bf16[512,1536]{1,0:T(8,128)(2,1)}, bf16[512,1536]{1,0:T(8,128)(2,1)S(1)}, u32[]{:S(2)}) copy-start(bf16[512,1536]{1,0:T(8,128)(2,1)S(1)} %collective-permute-done.3) | copy-start | bytes 4718596
  201.6 69.9 %collective-permute-start.5 = (bf16[512,1536]{1,0:T(8,128)(2,1)}, bf16[512,1536]{1,0:T(8,128)(2,1)}, u32[]{:S(2)}, u32[]{:S(2)}) collective-permute-start(bf16[512,1536]{1,0:T(8,128)(2,1)} %fusion.73), channel_id=1, source_target_pairs={{0,2},{2,0},{1,3},{3,1},{4,6},{6,4},{5,7},{7,5},{8,10},{10,8},{9,1... | collective-permute-start | bytes 4718600 | tf_op jit(solution)/shard_map/ppermute | solution.py:83
  242.0 153.5 %reduce-scatter.5.cloned.1.call-start = ((), (), s32[]{:S(2)}) async-start(), calls=%async_computation.5 | async-start | bytes 3538944 | tf_op jit(solution)/shard_map/reduce_scatter | solution.py:91
  242.5 62.7 %collective-permute-start.6 = (bf16[512,1536]{1,0:T(8,128)(2,1)}, bf16[512,1536]{1,0:T(8,128)(2,1)S(1)}, u32[]{:S(2)}, u32[]{:S(2)}) collective-permute-start(bf16[512,1536]{1,0:T(8,128)(2,1)} %fusion.79), channel_id=1, source_target_pairs={{0,2},{2,0},{1,3},{3,1},{4,6},{6,4},{5,7},{7,5},{8,10},{10,8},{9,1... | collective-permute-start | bytes 4718600 | tf_op jit(solution)/shard_map/ppermute | solution.py:83
  271.5 65.8 %collective-permute-start.7 = (bf16[512,1536]{1,0:T(8,128)(2,1)}, bf16[512,1536]{1,0:T(8,128)(2,1)}, u32[]{:S(2)}, u32[]{:S(2)}) collective-permute-start(bf16[512,1536]{1,0:T(8,128)(2,1)} %fusion.85), channel_id=1, source_target_pairs={{0,2},{2,0},{1,3},{3,1},{4,6},{6,4},{5,7},{7,5},{8,10},{10,8},{9,1... | collective-permute-start | bytes 4718600 | tf_op jit(solution)/shard_map/ppermute | solution.py:83
  288.2 16.9 %copy-start.3 = (bf16[512,1536]{1,0:T(8,128)(2,1)S(1)}, bf16[512,1536]{1,0:T(8,128)(2,1)}, u32[]{:S(2)}) copy-start(bf16[512,1536]{1,0:T(8,128)(2,1)} %fusion.76) | copy-start | bytes 4718596
  288.2 16.9 %copy-start.4 = (bf16[512,1536]{1,0:T(8,128)(2,1)S(1)}, bf16[512,1536]{1,0:T(8,128)(2,1)}, u32[]{:S(2)}) copy-start(bf16[512,1536]{1,0:T(8,128)(2,1)} %fusion.79) | copy-start | bytes 4718596
  288.2 16.9 %copy-start.8 = (bf16[512,1536]{1,0:T(8,128)(2,1)S(1)}, bf16[512,1536]{1,0:T(8,128)(2,1)}, u32[]{:S(2)}) copy-start(bf16[512,1536]{1,0:T(8,128)(2,1)} %copy-done.7) | copy-start | bytes 4718596
  302.9 34.4 %copy-start.6 = (bf16[512,1536]{1,0:T(8,128)(2,1)S(1)}, bf16[512,1536]{1,0:T(8,128)(2,1)}, u32[]{:S(2)}) copy-start(bf16[512,1536]{1,0:T(8,128)(2,1)} %copy-done.5) | copy-start | bytes 4718596
Sparse Core Ops, SparseCore 0:
  9.6 40.9 all-gather.2
  52.3 37.1 all-gather.4
  242.1 39.1 reduce-scatter.2
  356.3 39.1 reduce-scatter.4

commit v2 on v0

--- a/solution.py
+++ b/solution.py
@@ -1,6 +1,8 @@
 import jax
 import jax.numpy as jnp
 from jax import lax
+from jax.experimental import pallas as pl
+from jax.experimental.pallas import tpu as pltpu
 from jax.sharding import PartitionSpec as P
 
 gelu_const = 0.7978845608028654
@@ -69,6 +71,221 @@
     return (outputs, input_grad)
 
 
+def ordered(value, earlier):
+    return lax.optimization_barrier((value, earlier))[0]
+
+
+vmem_bytes = 48 * 1024 * 1024
+light = pl.CostEstimate(flops=1, bytes_accessed=1, transcendentals=0)
+
+
+def inner_kernel(seen_ref, weight_ref, out_ref):
+    made = inner_product(seen_ref[...], weight_ref[...])
+    out_ref[...] = made.astype(out_ref.dtype)
+
+
+def inner_call(seen, weight, piece, pieces):
+    tokens, depth = seen.shape
+    width = weight.shape[0] // pieces
+    tile = 256
+    blocks = width // tile
+    return pl.pallas_call(
+        inner_kernel,
+        grid=(blocks,),
+        out_shape=jax.ShapeDtypeStruct((tokens, width), jnp.bfloat16),
+        in_specs=[
+            pl.BlockSpec((tokens, depth), lambda i: (0, 0)),
+            pl.BlockSpec((tile, depth), lambda i: (piece * blocks + i, 0)),
+        ],
+        out_specs=pl.BlockSpec((tokens, tile), lambda i: (0, i)),
+        compiler_params=pltpu.CompilerParams(vmem_limit_bytes=vmem_bytes),
+        cost_estimate=light,
+    )(seen, weight)
+
+
+def outer_kernel(pairs, resumed, *refs):
+    shares, rest = refs[: 2 * pairs], refs[2 * pairs :]
+    weight_ref, out_ref = rest[0], rest[-1]
+
+    @pl.when(pl.program_id(0) == 0)
+    def begin():
+        out_ref[...] = rest[1][...] if resumed else jnp.zeros_like(out_ref)
+
+    sums = [
+        shares[2 * i][...].astype(jnp.float32) + shares[2 * i + 1][...].astype(jnp.float32)
+        for i in range(pairs)
+    ]
+    if pairs == 1:
+        share = gelu_value(sums[0])
+    else:
+        share = sums[0] * gelu_slope(sums[1])
+    out_ref[...] += outer_term(share.astype(jnp.bfloat16), weight_ref[...])
+
+
+def outer_call(total, shares, weight, piece):
+    tokens, width = shares[0].shape
+    columns = weight.shape[1]
+    tile = 512
+    blocks = width // tile
+    whole = pl.BlockSpec((tokens, columns), lambda i: (0, 0))
+    resumed = total is not None
+    return pl.pallas_call(
+        lambda *refs: outer_kernel(len(shares) // 2, resumed, *refs),
+        grid=(blocks,),
+        out_shape=jax.ShapeDtypeStruct((tokens, columns), jnp.float32),
+        in_specs=[pl.BlockSpec((tokens, tile), lambda i: (0, i))] * len(shares)
+        + [pl.BlockSpec((tile, columns), lambda i: (piece * blocks + i, 0))]
+        + [whole] * resumed,
+        out_specs=whole,
+        compiler_params=pltpu.CompilerParams(vmem_limit_bytes=vmem_bytes),
+        cost_estimate=light,
+    )(*shares, weight, *([total] * resumed))
+
+
+def place_kernel(chips, rows, chip_ref, total_ref, out_ref):
+    chip = chip_ref[0]
+    for step in range(chips):
+        start = pl.multiple_of(lax.rem(chip + step, chips) * rows, rows)
+        if step == 0:
+            block = jnp.zeros((rows, out_ref.shape[1]), out_ref.dtype)
+        else:
+            block = total_ref[(step - 1) * rows : step * rows, :].astype(out_ref.dtype)
+        out_ref[pl.ds(start, rows), :] = block
+
+
+def place_call(total, chip, chips, rows):
+    columns = total.shape[1]
+    tile = columns // 4
+    return pl.pallas_call(
+        lambda *refs: place_kernel(chips, rows, *refs),
+        grid=(4,),
+        out_shape=jax.ShapeDtypeStruct((chips * rows, columns), jnp.bfloat16),
+        in_specs=[
+            pl.BlockSpec(memory_space=pltpu.SMEM),
+            pl.BlockSpec((total.shape[0], tile), lambda i: (0, i)),
+        ],
+        out_specs=pl.BlockSpec((chips * rows, tile), lambda i: (0, i)),
+        compiler_params=pltpu.CompilerParams(vmem_limit_bytes=vmem_bytes),
+        cost_estimate=light,
+    )(jnp.reshape(chip, (1,)).astype(jnp.int32), total)
+
+
+swapped = [(0, 1), (1, 0)]
+
+
+def pair_body(chips, near_cut, far_cut, inputs, cotangent, up_weight, down_weight):
+    units = up_weight.shape[0]
+    rows = 2 * inputs.shape[0]
+    chip = lax.axis_index("gx")
+    others = [lax.rem(chip + step, chips) * rows for step in range(1, chips)]
+    sent = []
+
+    def swap(term):
+        if len(sent) >= 2:
+            term = ordered(term, sent[-2])
+        other = lax.ppermute(term, "gy", swapped)
+        sent.append(other)
+        return (term, other)
+
+    def near_rows(mine):
+        return jnp.concatenate([mine, lax.ppermute(mine, "gz", swapped)])
+
+    def far_rows(mine):
+        seen = lax.all_gather(mine, ("gx", "gz"), axis=0, tiled=True)
+        return jnp.concatenate(
+            [lax.dynamic_slice_in_dim(seen, start, rows, 0) for start in others]
+        )
+
+    last = [inputs]
+
+    def after(values, *earlier):
+        return lax.optimization_barrier((values, last[0]) + earlier)[0]
+
+    def scatter(total, *earlier):
+        placed = place_call(after(total, *earlier), chip, chips, rows)
+        last[0] = placed
+        return lax.psum_scatter(placed, ("gx", "gz"), scatter_dimension=0, tiled=True)
+
+    def term(seen, weight, piece, pieces, *earlier):
+        seen = after(seen, *earlier)
+        made = inner_call(seen, weight, piece, pieces)
+        last[0] = made
+        return made
+
+    def add_act(total, hidden, piece):
+        last[0] = outer_call(total, after(hidden[piece]), down_weight, piece)
+        return last[0]
+
+    def add_grad(total, slope, hidden, piece):
+        shares = after(slope[piece] + hidden[piece])
+        last[0] = outer_call(total, shares, up_weight, piece)
+        return last[0]
+
+    def finish(far, near):
+        near = near.astype(jnp.bfloat16)
+        half = rows // 2
+        other = lax.ppermute(near[half:], "gz", swapped)
+        total = far.astype(jnp.float32) + near[:half].astype(jnp.float32)
+        return (total + other.astype(jnp.float32)).astype(jnp.bfloat16)
+
+    near_inputs = near_rows(inputs)
+    far_inputs = far_rows(inputs)
+    near_cotangent = near_rows(ordered(cotangent, near_inputs))
+    far_cotangent = far_rows(ordered(cotangent, inputs))
+
+    near_hidden = [
+        swap(term(near_inputs, up_weight, piece, near_cut)) for piece in range(near_cut)
+    ]
+    near_terms = []
+
+    def near_term():
+        index = len(near_terms)
+        near_terms.append(term(near_cotangent, down_weight, index, near_cut))
+
+    near_term()
+    far_hidden, far_slope, near_slope = [], [], []
+    near_out, near_grad, far_out, far_grad = None, None, None, None
+    for piece in range(far_cut):
+        made = term(far_inputs, up_weight, piece, far_cut, sent[-2])
+        far_hidden.append(swap(made))
+        if piece == 1:
+            for index in range(near_cut):
+                near_out = add_act(near_out, near_hidden, index)
+            near_term()
+        if piece >= 2:
+            far_out = add_act(far_out, far_hidden, piece - 2)
+    for piece in range(far_cut):
+        if piece == 3:
+            far_outputs = scatter(far_out, sent[-2])
+        made = term(far_cotangent, down_weight, piece, far_cut, sent[-2])
+        far_slope.append(swap(made))
+        if piece < 2:
+            far_out = add_act(far_out, far_hidden, far_cut - 2 + piece)
+            if piece == 1:
+                near_term()
+        else:
+            far_grad = add_grad(far_grad, far_slope, far_hidden, piece - 2)
+    for piece in range(near_cut):
+        near_slope.append(swap(near_terms[piece]))
+        if piece < 2:
+            index = far_cut - 2 + piece
+            far_grad = add_grad(far_grad, far_slope, far_hidden, index)
+    far_gradient = scatter(far_grad)
+    for piece in range(near_cut):
+        near_grad = add_grad(near_grad, near_slope, near_hidden, piece)
+    return (finish(far_outputs, near_out), finish(far_gradient, near_grad))
+
+
+def chosen_body(mesh):
+    def run(inputs, cotangent, up_weight, down_weight):
+        sizes = mesh.shape
+        if sizes["gy"] != 2 or sizes["gz"] != 2 or up_weight.shape[0] % 6144 != 0:
+            return body(inputs, cotangent, up_weight, down_weight)
+        return pair_body(sizes["gx"], 3, 4, inputs, cotangent, up_weight, down_weight)
+
+    return run
+
+
 def solution(mesh):
     placed = (
         P(("groups", "gx", "gz"), "gy"),
@@ -77,7 +294,7 @@
         P(("gx", "gz"), "gy"),
     )
     return jax.shard_map(
-        body,
+        chosen_body(mesh),
         mesh=mesh,
         in_specs=placed,
         out_specs=(P(("groups", "gx", "gz"), "gy"), P(("groups", "gx", "gz"), "gy")),

time: 510 us -> 350 us (0.69)
  waiting for transfers between devices: 378 us -> 36.7 us
  Pallas kernels: 0 us -> 258 us
  matrix products: 109 us -> 0 us
  local copies, waits for them, and re-layouts: 0 us -> 17.1 us
  starting transfers between devices: 0.5 us -> 17.3 us
    pallas_call x0 -> x30, Pallas kernels: none -> 258 us  [the longest x14 129 us: outer_call(): pl.pallas_call(lambda *refs: outer_kernel(len(shares) // 2, resumed, *ref...]
    reduce_scatter x4 -> x2, waiting for transfers between devices: 188 us -> 0.02 us  [scatter(): lax.psum_scatter(placed, ('gx', 'gz'), scatter_dimension=0, tiled=True)]
    all_gather x4 -> x2, waiting for transfers between devices: 188 us -> 0.01 us  [far_rows(): seen = lax.all_gather(mine, ('gx', 'gz'), axis=0, tiled=True)]
    dot_general x4 -> x0, matrix products: 109 us -> none  [the longest x2 55.1 us: outer_term(): return jnp.dot(left, right, preferred_element_type=jnp.float32)]
    ppermute x0 -> x18, waiting for transfers between devices: none -> 35.3 us  [the longest x14 34.7 us: swap(): other = lax.ppermute(term, 'gy', swapped)]
    ppermute x0 -> x18, starting transfers between devices: none -> 17.1 us  [the longest x14 16 us: swap(): other = lax.ppermute(term, 'gy', swapped)]
    unnamed x0 -> x84, local copies, waits for them, and re-layouts: none -> 12.3 us
  transfers between devices with their start and end apart: 8 -> 22, of which waited for: 8 -> 7; matrix products, arithmetic and copies ran while one was open for 21% -> 2% of each run, Pallas kernels for 0% -> 73%
where the time goes in v2:
time: 350 us; the launch traced here: 348 us
  Pallas kernels  258 us (74%)
  waiting for transfers between devices  36.7 us (10%)
  starting transfers between devices  17.3 us (5%)
  local copies, waits for them, and re-layouts  17.1 us (5%)
  between operations  14.4 us (4%)
  other arithmetic  4.26 us (1%)
    pallas_call x14, Pallas kernels, outer_call(): pl.pallas_call(lambda *refs: outer_kernel(len(shares) // 2, resumed, *ref...  129 us
    pallas_call x14, Pallas kernels, inner_call(): pl.pallas_call(inner_kernel, grid=(blocks,), out_shape=jax.ShapeDtypeStru...  121 us
    ppermute x14, waiting for transfers between devices, swap(): other = lax.ppermute(term, 'gy', swapped)  34.7 us
    ppermute x14, starting transfers between devices, swap(): other = lax.ppermute(term, 'gy', swapped)  16 us
    unnamed x84, local copies, waits for them, and re-layouts  12.3 us
    pallas_call x2, Pallas kernels, place_call(): pl.pallas_call(lambda *refs: place_kernel(chips, rows, *refs), grid=(4,),...  7.88 us
  transfers between devices with their start and end apart: 22, of which 7 were waited for; matrix products, arithmetic and copies ran while one was open for 2% of the time, Pallas kernels for 73%

profile of v2, /device:TPU:0, one launch (start us, length us, event | category | flops | bytes accessed | tf_op | source)
XLA Modules:
  0.0 348.1 jit_solution(679263762262781697)
XLA Ops:
  7.2 0.7 all-gather.3.cloned.1.call-update
  8.0 0.7 all-gather.5.cloned.1.call-update
  9.2 1.0 constant_dynamic-update-slice_fusion.1
  11.3 9.3 %shard_map.59.refs_0_.refs_2_ = bf16[128,2048]{1,0:T(8,128)(2,1)S(1)} custom-call(bf16[128,3072]{1,0:T(8,128)(2,1)S(1)} %constant_dynamic-update-slice_fusion.seen_ref, bf16[6144,3072]{1,0:T(8,128)(2,1)} %refs_4_.13), custom_call_target="tpu_custom_call" | custom-call | flops 1 | bytes 1 | tf_op jit(solution)/shard_map/pallas_call | solution.py:92
  20.6 2.7 collective-permute-start.4
  23.3 9.2 %shard_map.60.refs_0_.refs_2_ = bf16[128,2048]{1,0:T(8,128)(2,1)S(1)} custom-call(bf16[128,3072]{1,0:T(8,128)(2,1)S(1)} %constant_dynamic-update-slice_fusion.seen_ref, bf16[6144,3072]{1,0:T(8,128)(2,1)} %refs_4_.13), custom_call_target="tpu_custom_call" | custom-call | flops 1 | bytes 1 | tf_op jit(solution)/shard_map/pallas_call | solution.py:92
  32.8 9.3 %shard_map.61.refs_0_.refs_2_ = bf16[128,2048]{1,0:T(8,128)(2,1)S(1)} custom-call(bf16[128,3072]{1,0:T(8,128)(2,1)S(1)} %constant_dynamic-update-slice_fusion.seen_ref, bf16[6144,3072]{1,0:T(8,128)(2,1)} %refs_4_.13), custom_call_target="tpu_custom_call" | custom-call | flops 1 | bytes 1 | tf_op jit(solution)/shard_map/pallas_call | solution.py:92
  42.2 1.2 constant_dynamic-update-slice_fusion.2.seen_ref
  43.4 9.6 %shard_map.62.refs_0_ = bf16[128,2048]{1,0:T(8,128)(2,1)S(1)} custom-call(bf16[128,3072]{1,0:T(8,128)(2,1)S(1)} %constant_dynamic-update-slice_fusion.2.seen_ref, bf16[6144,3072]{1,0:T(8,128)(2,1)} %weight_ref.27), custom_call_target="tpu_custom_call" | custom-call | flops 1 | bytes 1 | tf_op jit(solution)/shard_map/pallas_call | solution.py:92
  53.0 0.8 copy-done.30
  53.8 0.9 copy-done.24
  54.6 1.8 collective-permute-start.5
  56.4 1.8 constant_dynamic-slice_fusion.5
  58.4 7.9 %shard_map.63.refs_0_.refs_2_ = bf16[384,1536]{1,0:T(8,128)(2,1)S(1)} custom-call(bf16[384,3072]{1,0:T(8,128)(2,1)S(1)} %pad_maximum_fusion.seen_ref, bf16[6144,3072]{1,0:T(8,128)(2,1)} %refs_4_.13), custom_call_target="tpu_custom_call" | custom-call | flops 1 | bytes 1 | tf_op jit(solution)/shard_map/pallas_call | solution.py:92
  66.5 2.2 collective-permute-done.5.refs_1_.refs_3_
  68.7 0.8 copy-done.27
  69.5 7.8 %shard_map.64.refs_0_.refs_2_ = bf16[384,1536]{1,0:T(8,128)(2,1)S(1)} custom-call(bf16[384,3072]{1,0:T(8,128)(2,1)S(1)} %pad_maximum_fusion.seen_ref, bf16[6144,3072]{1,0:T(8,128)(2,1)} %refs_4_.13), custom_call_target="tpu_custom_call" | custom-call | flops 1 | bytes 1 | tf_op jit(solution)/shard_map/pallas_call | solution.py:92
  77.4 2.6 collective-permute-start.6
  79.9 6.4 %shard_map.65.refs_3_ = f32[128,3072]{1,0:T(8,128)S(1)} custom-call(bf16[128,2048]{1,0:T(8,128)(2,1)S(1)} %shard_map.59.refs_0_.refs_2_, bf16[128,2048]{1,0:T(8,128)(2,1)S(1)} %copy-done.25, bf16[6144,3072]{1,0:T(8,128)(2,1)} %weight_ref.27), custom_call_target="tpu_custom_call" | custom-call | flops 1 | bytes 1 | tf_op jit(solution)/shard_map/pallas_call | solution.py:132
  86.4 6.6 %shard_map.66.refs_3_ = f32[128,3072]{1,0:T(8,128)S(1)} custom-call(bf16[128,2048]{1,0:T(8,128)(2,1)S(1)} %copy-done.11, bf16[128,2048]{1,0:T(8,128)(2,1)} %collective-permute-done.2.refs_1_.refs_3_, bf16[6144,3072]{1,0:T(8,128)(2,1)} %weight_ref.27, f32[128,3072]{1,0:T(8,128)S(1)} %shard_map.65.refs_3_), custom_call_target="tpu_custom_call" | custom-call | flops 1 | bytes 1 | tf_op jit(solution)/shard_map/pallas_call | solution.py:132
  93.0 6.3 %shard_map.67 = f32[128,3072]{1,0:T(8,128)S(1)} custom-call(bf16[128,2048]{1,0:T(8,128)(2,1)S(1)} %copy-done.8, bf16[128,2048]{1,0:T(8,128)(2,1)S(1)} %copy-done.28, bf16[6144,3072]{1,0:T(8,128)(2,1)} %weight_ref.27, f32[128,3072]{1,0:T(8,128)S(1)} %shard_map.66.refs_3_), custom_call_target="tpu_custom_call" | custom-call | flops 1 | bytes 1 | tf_op jit(solution)/shard_map/pallas_call | solution.py:132
  99.4 1.1 copy-done.5
  100.5 9.2 %shard_map.68.refs_0_ = bf16[128,2048]{1,0:T(8,128)(2,1)S(1)} custom-call(bf16[128,3072]{1,0:T(8,128)(2,1)S(1)} %constant_dynamic-update-slice_fusion.2.seen_ref, bf16[6144,3072]{1,0:T(8,128)(2,1)} %weight_ref.27), custom_call_target="tpu_custom_call" | custom-call | flops 1 | bytes 1 | tf_op jit(solution)/shard_map/pallas_call | solution.py:92
  109.8 9.2 %shard_map.69.refs_0_.refs_2_ = bf16[384,1536]{1,0:T(8,128)(2,1)} custom-call(bf16[384,3072]{1,0:T(8,128)(2,1)S(1)} %pad_maximum_fusion.seen_ref, bf16[6144,3072]{1,0:T(8,128)(2,1)} %refs_4_.13), custom_call_target="tpu_custom_call" | custom-call | flops 1 | bytes 1 | tf_op jit(solution)/shard_map/pallas_call | solution.py:92
  119.1 9.4 %shard_map.70.refs_3_ = f32[384,3072]{1,0:T(8,128)} custom-call(bf16[384,1536]{1,0:T(8,128)(2,1)S(1)} %shard_map.63.refs_0_.refs_2_, bf16[384,1536]{1,0:T(8,128)(2,1)S(1)} %collective-permute-done.3.refs_1_.refs_3_, bf16[6144,3072]{1,0:T(8,128)(2,1)} %weight_ref.27), custom_call_target="tpu_custom_call" | custom-call | flops 1 | bytes 1 | tf_op jit(solution)/shard_map/pallas_call | solution.py:132
  128.5 9.0 %shard_map.71.refs_0_.refs_2_ = bf16[384,1536]{1,0:T(8,128)(2,1)} custom-call(bf16[384,3072]{1,0:T(8,128)(2,1)S(1)} %pad_maximum_fusion.seen_ref, bf16[6144,3072]{1,0:T(8,128)(2,1)} %refs_4_.13), custom_call_target="tpu_custom_call" | custom-call | flops 1 | bytes 1 | tf_op jit(solution)/shard_map/pallas_call | solution.py:92
  137.6 1.9 collective-permute-start.7
  139.5 1.8 constant_dynamic-slice_fusion.2
  141.5 1.1 copy-done.16
  142.6 10.9 %shard_map.72.refs_3_ = f32[384,3072]{1,0:T(8,128)} custom-call(bf16[384,1536]{1,0:T(8,128)(2,1)S(1)} %shard_map.64.refs_0_.refs_2_, bf16[384,1536]{1,0:T(8,128)(2,1)S(1)} %copy-done.16, bf16[6144,3072]{1,0:T(8,128)(2,1)} %weight_ref.27, f32[384,3072]{1,0:T(8,128)} %shard_map.70.refs_3_), custom_call_target="tpu_custom_call" | custom-call | flops 1 | bytes 1 | tf_op jit(solution)/shard_map/pallas_call | solution.py:132
  153.4 7.8 %shard_map.73.refs_0_ = bf16[384,1536]{1,0:T(8,128)(2,1)S(1)} custom-call(bf16[384,3072]{1,0:T(8,128)(2,1)S(1)} %pad_maximum_fusion.1.seen_ref, bf16[6144,3072]{1,0:T(8,128)(2,1)} %weight_ref.27), custom_call_target="tpu_custom_call" | custom-call | flops 1 | bytes 1 | tf_op jit(solution)/shard_map/pallas_call | solution.py:92
  161.3 11.5 %shard_map.74.refs_3_ = f32[384,3072]{1,0:T(8,128)} custom-call(bf16[384,1536]{1,0:T(8,128)(2,1)} %shard_map.69.refs_0_.refs_2_, bf16[384,1536]{1,0:T(8,128)(2,1)} %collective-permute-done.8.refs_1_.refs_3_, bf16[6144,3072]{1,0:T(8,128)(2,1)} %weight_ref.27, f32[384,3072]{1,0:T(8,128)} %shard_map.72.refs_3_), custom_call_target="tpu_custom_call" | custom-call | flops 1 | bytes 1 | tf_op jit(solution)/shard_map/pallas_call | solution.py:132
  173.5 7.8 %shard_map.75.refs_0_ = bf16[384,1536]{1,0:T(8,128)(2,1)S(1)} custom-call(bf16[384,3072]{1,0:T(8,128)(2,1)S(1)} %pad_maximum_fusion.1.seen_ref, bf16[6144,3072]{1,0:T(8,128)(2,1)} %weight_ref.27), custom_call_target="tpu_custom_call" | custom-call | flops 1 | bytes 1 | tf_op jit(solution)/shard_map/pallas_call | solution.py:92
  181.3 1.2 collective-permute-start.10
  182.5 11.4 %shard_map.76.refs_1_ = f32[384,3072]{1,0:T(8,128)} custom-call(bf16[384,1536]{1,0:T(8,128)(2,1)} %shard_map.71.refs_0_.refs_2_, bf16[384,1536]{1,0:T(8,128)(2,1)} %collective-permute-done.7.refs_1_.refs_3_, bf16[6144,3072]{1,0:T(8,128)(2,1)} %weight_ref.27, f32[384,3072]{1,0:T(8,128)} %shard_map.74.refs_3_), custom_call_target="tpu_custom_call" | custom-call | flops 1 | bytes 1 | tf_op jit(solution)/shard_map/pallas_call | solution.py:132
  193.9 9.2 %shard_map.77.refs_0_ = bf16[128,2048]{1,0:T(8,128)(2,1)S(1)} custom-call(bf16[128,3072]{1,0:T(8,128)(2,1)S(1)} %copy-done.4, bf16[6144,3072]{1,0:T(8,128)(2,1)} %weight_ref.27), custom_call_target="tpu_custom_call" | custom-call | flops 1 | bytes 1 | tf_op jit(solution)/shard_map/pallas_call | solution.py:92
  203.2 0.8 copy-done.34
  204.0 7.9 %shard_map.78.refs_0_ = bf16[384,1536]{1,0:T(8,128)(2,1)S(1)} custom-call(bf16[384,3072]{1,0:T(8,128)(2,1)S(1)} %pad_maximum_fusion.1.seen_ref, bf16[6144,3072]{1,0:T(8,128)(2,1)} %weight_ref.27), custom_call_target="tpu_custom_call" | custom-call | flops 1 | bytes 1 | tf_op jit(solution)/shard_map/pallas_call | solution.py:92
  211.9 1.0 copy-done.22
  213.0 10.2 %shard_map.79.refs_5_ = f32[384,3072]{1,0:T(8,128)} custom-call(bf16[384,1536]{1,0:T(8,128)(2,1)S(1)} %shard_map.73.refs_0_, bf16[384,1536]{1,0:T(8,128)(2,1)S(1)} %collective-permute-done.9.refs_1_, bf16[384,1536]{1,0:T(8,128)(2,1)S(1)} %copy-done.2, bf16[384,1536]{1,0:T(8,128)(2,1)S(1)} %copy-done.19, bf16[6144,3072]{1,0:T(8,128)(2,1)} %refs_4_.13), custom_call_target="tpu_custom_call" | custom-call | flops 1 | bytes 1 | tf_op jit(solution)/shard_map/pallas_call | solution.py:132
  223.2 1.1 copy-done.36
  224.2 3.2 shard_map.80
  227.5 1.6 copy-done
  229.2 0.9 collective-permute-start.13
  230.2 7.9 %shard_map.81.refs_0_ = bf16[384,1536]{1,0:T(8,128)(2,1)S(1)} custom-call(bf16[384,3072]{1,0:T(8,128)(2,1)S(1)} %pad_maximum_fusion.1.seen_ref, bf16[6144,3072]{1,0:T(8,128)(2,1)} %weight_ref.27), custom_call_target="tpu_custom_call" | custom-call | flops 1 | bytes 1 | tf_op jit(solution)/shard_map/pallas_call | solution.py:92
  238.1 1.3 collective-permute-start.12
  239.4 11.8 %shard_map.82.refs_5_ = f32[384,3072]{1,0:T(8,128)} custom-call(bf16[384,1536]{1,0:T(8,128)(2,1)S(1)} %copy-done.21, bf16[384,1536]{1,0:T(8,128)(2,1)S(1)} %copy-done.37, bf16[384,1536]{1,0:T(8,128)(2,1)S(1)} %shard_map.64.refs_0_.refs_2_, bf16[384,1536]{1,0:T(8,128)(2,1)S(1)} %copy-done.17, bf16[6144,3072]{1,0:T(8,128)(2,1)} %refs_4_.13, ...), custom_call_target="tpu_custom_call" | custom-call | flops 1 | bytes 1 | tf_op jit(solution)/shard_map/pallas_call | solution.py:132
  251.2 7.2 %collective-permute-done.13.refs_1_ = bf16[384,1536]{1,0:T(8,128)(2,1)S(1)} collective-permute-done((bf16[384,1536]{1,0:T(8,128)(2,1)}, bf16[384,1536]{1,0:T(8,128)(2,1)S(1)}, u32[]{:S(2)}, u32[]{:S(2)}) %collective-permute-start.13) | collective-permute-done | bytes 1179680 | tf_op jit(solution)/shard_map/ppermute | solution.py:186
  258.4 12.2 %shard_map.83.refs_5_ = f32[384,3072]{1,0:T(8,128)} custom-call(bf16[384,1536]{1,0:T(8,128)(2,1)S(1)} %copy-done.23, bf16[384,1536]{1,0:T(8,128)(2,1)S(1)} %collective-permute-done.13.refs_1_, bf16[384,1536]{1,0:T(8,128)(2,1)} %shard_map.69.refs_0_.refs_2_, bf16[384,1536]{1,0:T(8,128)(2,1)} %collective-permute-done.8.refs_1_.refs_3_, ...), custom_call_target="tpu_custom_call" | custom-call | flops 1 | bytes 1 | tf_op jit(solution)/shard_map/pallas_call | solution.py:132
  270.6 8.6 %collective-permute-done.12.refs_1_ = bf16[384,1536]{1,0:T(8,128)(2,1)S(1)} collective-permute-done((bf16[384,1536]{1,0:T(8,128)(2,1)S(1)}, bf16[384,1536]{1,0:T(8,128)(2,1)S(1)}, u32[]{:S(2)}, u32[]{:S(2)}) %collective-permute-start.12) | collective-permute-done | bytes 1179680 | tf_op jit(solution)/shard_map/ppermute | solution.py:186
  279.2 12.0 %shard_map.84.refs_1_ = f32[384,3072]{1,0:T(8,128)} custom-call(bf16[384,1536]{1,0:T(8,128)(2,1)S(1)} %shard_map.81.refs_0_, bf16[384,1536]{1,0:T(8,128)(2,1)S(1)} %collective-permute-done.12.refs_1_, bf16[384,1536]{1,0:T(8,128)(2,1)} %shard_map.71.refs_0_.refs_2_, bf16[384,1536]{1,0:T(8,128)(2,1)} %collective-permute-done.7.refs_1_.refs_3_, ...), custom_call_target="tpu_custom_call" | custom-call | flops 1 | bytes 1 | tf_op jit(solution)/shard_map/pallas_call | solution.py:132
  291.2 4.6 %shard_map.85 = bf16[512,3072]{1,0:T(8,128)(2,1)} custom-call(s32[1]{0:T(128)} %bitcast.refs_0_, f32[384,3072]{1,0:T(8,128)} %shard_map.84.refs_1_), custom_call_target="tpu_custom_call" | custom-call | flops 1 | bytes 1 | tf_op jit(solution)/shard_map/pallas_call | solution.py:159
  295.9 1.0 copy-done.31
  296.9 0.8 collective-permute-start.14
  297.8 1.2 collective-permute-start.16
  299.0 12.8 %collective-permute-done.14.refs_1_ = bf16[128,2048]{1,0:T(8,128)(2,1)S(1)} collective-permute-done((bf16[128,2048]{1,0:T(8,128)(2,1)S(1)}, bf16[128,2048]{1,0:T(8,128)(2,1)S(1)}, u32[]{:S(2)}, u32[]{:S(2)}) %collective-permute-start.14) | collective-permute-done | bytes 524320 | tf_op jit(solution)/shard_map/ppermute | solution.py:186
  311.8 0.8 collective-permute-start.15
  312.9 7.0 %shard_map.86.refs_5_ = f32[128,3072]{1,0:T(8,128)S(1)} custom-call(bf16[128,2048]{1,0:T(8,128)(2,1)S(1)} %copy-done.31, bf16[128,2048]{1,0:T(8,128)(2,1)S(1)} %collective-permute-done.14.refs_1_, bf16[128,2048]{1,0:T(8,128)(2,1)S(1)} %copy-done.14, bf16[128,2048]{1,0:T(8,128)(2,1)S(1)} %copy-done.26, bf16[6144,3072]{1,0:T(8,128)(2,1)} %refs_4_.13), custom_call_target="tpu_custom_call" | custom-call | flops 1 | bytes 1 | tf_op jit(solution)/shard_map/pallas_call | solution.py:132
  319.9 3.2 collective-permute-done.16.refs_1_
  323.0 6.9 %shard_map.87.refs_5_ = f32[128,3072]{1,0:T(8,128)S(1)} custom-call(bf16[128,2048]{1,0:T(8,128)(2,1)S(1)} %copy-done.33, bf16[128,2048]{1,0:T(8,128)(2,1)S(1)} %collective-permute-done.16.refs_1_, bf16[128,2048]{1,0:T(8,128)(2,1)S(1)} %copy-done.12, bf16[128,2048]{1,0:T(8,128)(2,1)} %collective-permute-done.2.refs_1_.refs_3_, bf16[6144,3072]{1,0:T(8,128)(2,1)} %refs_4_.13, ...), custom_call_target="tpu_custom_call" | custom-call | flops 1 | bytes 1 | tf_op jit(solution)/shard_map/pallas_call | solution.py:132
  330.0 6.7 %shard_map.88 = f32[128,3072]{1,0:T(8,128)S(1)} custom-call(bf16[128,2048]{1,0:T(8,128)(2,1)S(1)} %copy-done.35, bf16[128,2048]{1,0:T(8,128)(2,1)S(1)} %collective-permute-done.15.refs_1_, bf16[128,2048]{1,0:T(8,128)(2,1)S(1)} %copy-done.9, bf16[128,2048]{1,0:T(8,128)(2,1)S(1)} %copy-done.29, bf16[6144,3072]{1,0:T(8,128)(2,1)} %refs_4_.13, ...), custom_call_target="tpu_custom_call" | custom-call | flops 1 | bytes 1 | tf_op jit(solution)/shard_map/pallas_call | solution.py:132
  337.0 0.9 copy-done.39
  337.8 1.9 add_convert_fusion.1
  339.7 1.9 add_convert_fusion
  (110 shorter events, 4.0 us)
Async XLA Ops:
  7.2 3.7 %copy-start.40 = (bf16[64,3072]{1,0:T(8,128)(2,1)S(1)}, bf16[64,3072]{1,0:T(8,128)(2,1)}, u32[]{:S(2)}) copy-start(bf16[64,3072]{1,0:T(8,128)(2,1)} %param.5) | copy-start | bytes 1179652
  7.2 49.2 %all-gather.3.cloned.1.call-start = ((), (), s32[]{:S(2)}) async-start(), calls=%async_computation.2 | async-start | bytes 3538944 | tf_op jit(solution)/shard_map/all_gather | solution.py:194
  7.9 131.6 %all-gather.5.cloned.1.call-start = ((), (), s32[]{:S(2)}) async-start(), calls=%async_computation.3 | async-start | bytes 3538944 | tf_op jit(solution)/shard_map/all_gather | solution.py:194
  8.7 328.3 %reduce-scatter.3.cloned.1.call-start = ((), (), s32[]{:S(2)}) async-start(), calls=%async_computation.4 | async-start | bytes 3538944 | tf_op jit(solution)/shard_map/reduce_scatter | solution.py:207
  8.7 2.1 collective-permute-start
  10.8 31.4 %collective-permute-start.1 = (bf16[64,3072]{1,0:T(8,128)(2,1)S(1)}, bf16[64,3072]{1,0:T(8,128)(2,1)}, u32[]{:S(2)}, u32[]{:S(2)}) collective-permute-start(bf16[64,3072]{1,0:T(8,128)(2,1)S(1)} %copy-done.40), channel_id=1, source_target_pairs={{0,1},{1,0},{2,3},{3,2},{4,5},{5,4},{6,7},{7,6},{8,9},{9,8},{10,11... | collective-permute-start | bytes 1179656 | tf_op jit(solution)/shard_map/ppermute | solution.py:191
  20.6 59.4 %copy-start.13 = (bf16[128,2048]{1,0:T(8,128)(2,1)}, bf16[128,2048]{1,0:T(8,128)(2,1)S(1)}, u32[]{:S(2)}) copy-start(bf16[128,2048]{1,0:T(8,128)(2,1)S(1)} %shard_map.59.refs_0_.refs_2_) | copy-start | bytes 1572868
  20.6 33.2 %collective-permute-start.4 = (bf16[128,2048]{1,0:T(8,128)(2,1)S(1)}, bf16[128,2048]{1,0:T(8,128)(2,1)S(1)}, u32[]{:S(2)}, u32[]{:S(2)}) collective-permute-start(bf16[128,2048]{1,0:T(8,128)(2,1)S(1)} %shard_map.59.refs_0_.refs_2_), channel_id=1, source_target_pairs={{0,2},{2,0},{1,3},{3,1},{4,6},{6,4},{5,7},{7,5},{8,10},{10,8},{9,1... | collective-permute-start | bytes 1572872 | tf_op jit(solution)/shard_map/ppermute | solution.py:186
  32.5 9.6 %copy-start.10 = (bf16[128,2048]{1,0:T(8,128)(2,1)}, bf16[128,2048]{1,0:T(8,128)(2,1)S(1)}, u32[]{:S(2)}) copy-start(bf16[128,2048]{1,0:T(8,128)(2,1)S(1)} %shard_map.60.refs_0_.refs_2_) | copy-start | bytes 1572868
  32.6 25.9 %collective-permute-start.2 = (bf16[128,2048]{1,0:T(8,128)(2,1)S(1)}, bf16[128,2048]{1,0:T(8,128)(2,1)}, u32[]{:S(2)}, u32[]{:S(2)}) collective-permute-start(bf16[128,2048]{1,0:T(8,128)(2,1)S(1)} %shard_map.60.refs_0_.refs_2_), channel_id=1, source_target_pairs={{0,2},{2,0},{1,3},{3,1},{4,6},{6,4},{5,7},{7,5},{8,10},{10,8},{9,1... | collective-permute-start | bytes 1572872 | tf_op jit(solution)/shard_map/ppermute | solution.py:186
  42.2 11.6 %copy-start.7 = (bf16[128,2048]{1,0:T(8,128)(2,1)}, bf16[128,2048]{1,0:T(8,128)(2,1)S(1)}, u32[]{:S(2)}) copy-start(bf16[128,2048]{1,0:T(8,128)(2,1)S(1)} %shard_map.61.refs_0_.refs_2_) | copy-start | bytes 1572868
  43.4 56.0 %copy-start.3 = (bf16[128,3072]{1,0:T(8,128)(2,1)}, bf16[128,3072]{1,0:T(8,128)(2,1)S(1)}, u32[]{:S(2)}) copy-start(bf16[128,3072]{1,0:T(8,128)(2,1)S(1)} %constant_dynamic-update-slice_fusion.2.seen_ref) | copy-start | bytes 2359300
  53.0 0.8 copy-start.30
  53.8 0.9 copy-start.24
  54.6 14.1 %collective-permute-start.5 = (bf16[128,2048]{1,0:T(8,128)(2,1)S(1)}, bf16[128,2048]{1,0:T(8,128)(2,1)S(1)}, u32[]{:S(2)}, u32[]{:S(2)}) collective-permute-start(bf16[128,2048]{1,0:T(8,128)(2,1)S(1)} %shard_map.61.refs_0_.refs_2_), channel_id=1, source_target_pairs={{0,2},{2,0},{1,3},{3,1},{4,6},{6,4},{5,7},{7,5},{8,10},{10,8},{9,1... | collective-permute-start | bytes 1572872 | tf_op jit(solution)/shard_map/ppermute | solution.py:186
  66.3 52.8 %copy-start.1 = (bf16[384,1536]{1,0:T(8,128)(2,1)}, bf16[384,1536]{1,0:T(8,128)(2,1)S(1)}, u32[]{:S(2)}) copy-start(bf16[384,1536]{1,0:T(8,128)(2,1)S(1)} %shard_map.63.refs_0_.refs_2_) | copy-start | bytes 3538948
  66.3 13.6 %copy-start.25 = (bf16[128,2048]{1,0:T(8,128)(2,1)S(1)}, bf16[128,2048]{1,0:T(8,128)(2,1)}, u32[]{:S(2)}) copy-start(bf16[128,2048]{1,0:T(8,128)(2,1)} %copy-done.24) | copy-start | bytes 1572868
  66.3 43.5 %collective-permute-start.3 = (bf16[384,1536]{1,0:T(8,128)(2,1)S(1)}, bf16[384,1536]{1,0:T(8,128)(2,1)S(1)}, u32[]{:S(2)}, u32[]{:S(2)}) collective-permute-start(bf16[384,1536]{1,0:T(8,128)(2,1)S(1)} %shard_map.63.refs_0_.refs_2_), channel_id=1, source_target_pairs={{0,2},{2,0},{1,3},{3,1},{4,6},{6,4},{5,7},{7,5},{8,10},{10,8},{9,1... | collective-permute-start | bytes 3538952 | tf_op jit(solution)/shard_map/ppermute | solution.py:186
  68.7 0.8 copy-start.27
  77.4 9.0 %copy-start.11 = (bf16[128,2048]{1,0:T(8,128)(2,1)S(1)}, bf16[128,2048]{1,0:T(8,128)(2,1)}, u32[]{:S(2)}) copy-start(bf16[128,2048]{1,0:T(8,128)(2,1)} %copy-done.10) | copy-start | bytes 1572868
  77.4 51.2 %collective-permute-start.6 = (bf16[384,1536]{1,0:T(8,128)(2,1)S(1)}, bf16[384,1536]{1,0:T(8,128)(2,1)S(1)}, u32[]{:S(2)}, u32[]{:S(2)}) collective-permute-start(bf16[384,1536]{1,0:T(8,128)(2,1)S(1)} %shard_map.64.refs_0_.refs_2_), channel_id=1, source_target_pairs={{0,2},{2,0},{1,3},{3,1},{4,6},{6,4},{5,7},{7,5},{8,10},{10,8},{9,1... | collective-permute-start | bytes 3538952 | tf_op jit(solution)/shard_map/ppermute | solution.py:186
  86.4 6.6 %copy-start.8 = (bf16[128,2048]{1,0:T(8,128)(2,1)S(1)}, bf16[128,2048]{1,0:T(8,128)(2,1)}, u32[]{:S(2)}) copy-start(bf16[128,2048]{1,0:T(8,128)(2,1)} %copy-done.7) | copy-start | bytes 1572868
  86.4 6.6 %copy-start.28 = (bf16[128,2048]{1,0:T(8,128)(2,1)S(1)}, bf16[128,2048]{1,0:T(8,128)(2,1)}, u32[]{:S(2)}) copy-start(bf16[128,2048]{1,0:T(8,128)(2,1)} %copy-done.27) | copy-start | bytes 1572868
  99.4 1.2 copy-start.5
  109.8 9.2 %copy-start.32 = (bf16[128,2048]{1,0:T(8,128)(2,1)}, bf16[128,2048]{1,0:T(8,128)(2,1)S(1)}, u32[]{:S(2)}) copy-start(bf16[128,2048]{1,0:T(8,128)(2,1)S(1)} %shard_map.68.refs_0_) | copy-start | bytes 1572868
  109.8 9.3 %copy-start.18 = (bf16[384,1536]{1,0:T(8,128)(2,1)}, bf16[384,1536]{1,0:T(8,128)(2,1)S(1)}, u32[]{:S(2)}) copy-start(bf16[384,1536]{1,0:T(8,128)(2,1)S(1)} %collective-permute-done.3.refs_1_.refs_3_) | copy-start | bytes 3538948
  119.0 34.4 %collective-permute-start.8 = (bf16[384,1536]{1,0:T(8,128)(2,1)}, bf16[384,1536]{1,0:T(8,128)(2,1)}, u32[]{:S(2)}, u32[]{:S(2)}) collective-permute-start(bf16[384,1536]{1,0:T(8,128)(2,1)} %shard_map.69.refs_0_.refs_2_), channel_id=1, source_target_pairs={{0,2},{2,0},{1,3},{3,1},{4,6},{6,4},{5,7},{7,5},{8,10},{10,8},{9,1... | collective-permute-start | bytes 3538952 | tf_op jit(solution)/shard_map/ppermute | solution.py:186
  128.5 9.0 %copy-start.15 = (bf16[384,1536]{1,0:T(8,128)(2,1)}, bf16[384,1536]{1,0:T(8,128)(2,1)S(1)}, u32[]{:S(2)}) copy-start(bf16[384,1536]{1,0:T(8,128)(2,1)S(1)} %collective-permute-done.6.refs_1_.refs_3_) | copy-start | bytes 3538948
  137.6 36.0 %collective-permute-start.7 = (bf16[384,1536]{1,0:T(8,128)(2,1)}, bf16[384,1536]{1,0:T(8,128)(2,1)}, u32[]{:S(2)}, u32[]{:S(2)}) collective-permute-start(bf16[384,1536]{1,0:T(8,128)(2,1)} %shard_map.71.refs_0_.refs_2_), channel_id=1, source_target_pairs={{0,2},{2,0},{1,3},{3,1},{4,6},{6,4},{5,7},{7,5},{8,10},{10,8},{9,1... | collective-permute-start | bytes 3538952 | tf_op jit(solution)/shard_map/ppermute | solution.py:186
  141.3 1.3 copy-start.16
  161.2 42.8 %collective-permute-start.9 = (bf16[384,1536]{1,0:T(8,128)(2,1)S(1)}, bf16[384,1536]{1,0:T(8,128)(2,1)S(1)}, u32[]{:S(2)}, u32[]{:S(2)}) collective-permute-start(bf16[384,1536]{1,0:T(8,128)(2,1)S(1)} %shard_map.73.refs_0_), channel_id=1, source_target_pairs={{0,2},{2,0},{1,3},{3,1},{4,6},{6,4},{5,7},{7,5},{8,10},{10,8},{9,1... | collective-permute-start | bytes 3538952 | tf_op jit(solution)/shard_map/ppermute | solution.py:186
  181.3 12.6 %copy-start.20 = (bf16[384,1536]{1,0:T(8,128)(2,1)}, bf16[384,1536]{1,0:T(8,128)(2,1)S(1)}, u32[]{:S(2)}) copy-start(bf16[384,1536]{1,0:T(8,128)(2,1)S(1)} %shard_map.75.refs_0_) | copy-start | bytes 3538948
  181.3 12.6 %copy-start.4 = (bf16[128,3072]{1,0:T(8,128)(2,1)S(1)}, bf16[128,3072]{1,0:T(8,128)(2,1)}, u32[]{:S(2)}) copy-start(bf16[128,3072]{1,0:T(8,128)(2,1)} %copy-done.3) | copy-start | bytes 2359300
  181.3 41.8 %collective-permute-start.10 = (bf16[384,1536]{1,0:T(8,128)(2,1)S(1)}, bf16[384,1536]{1,0:T(8,128)(2,1)S(1)}, u32[]{:S(2)}, u32[]{:S(2)}) collective-permute-start(bf16[384,1536]{1,0:T(8,128)(2,1)S(1)} %shard_map.75.refs_0_), channel_id=1, source_target_pairs={{0,2},{2,0},{1,3},{3,1},{4,6},{6,4},{5,7},{7,5},{8,10},{10,8},{9,1... | collective-permute-start | bytes 3538952 | tf_op jit(solution)/shard_map/ppermute | solution.py:186
  203.2 0.8 copy-start.34
  204.0 9.0 %copy-start.2 = (bf16[384,1536]{1,0:T(8,128)(2,1)S(1)}, bf16[384,1536]{1,0:T(8,128)(2,1)}, u32[]{:S(2)}) copy-start(bf16[384,1536]{1,0:T(8,128)(2,1)} %copy-done.1) | copy-start | bytes 3538948
  204.0 9.0 %copy-start.19 = (bf16[384,1536]{1,0:T(8,128)(2,1)S(1)}, bf16[384,1536]{1,0:T(8,128)(2,1)}, u32[]{:S(2)}) copy-start(bf16[384,1536]{1,0:T(8,128)(2,1)} %copy-done.18) | copy-start | bytes 3538948
  211.9 1.0 copy-start.22
  223.2 1.1 copy-start.36
  227.5 1.6 copy-start
  229.1 110.6 %reduce-scatter.5.cloned.1.call-start = ((), (), s32[]{:S(2)}) async-start(), calls=%async_computation.5 | async-start | bytes 3538944 | tf_op jit(solution)/shard_map/reduce_scatter | solution.py:207
  229.2 10.2 %copy-start.17 = (bf16[384,1536]{1,0:T(8,128)(2,1)S(1)}, bf16[384,1536]{1,0:T(8,128)(2,1)}, u32[]{:S(2)}) copy-start(bf16[384,1536]{1,0:T(8,128)(2,1)} %copy-done.15) | copy-start | bytes 3538948
  229.2 10.2 %copy-start.21 = (bf16[384,1536]{1,0:T(8,128)(2,1)S(1)}, bf16[384,1536]{1,0:T(8,128)(2,1)}, u32[]{:S(2)}) copy-start(bf16[384,1536]{1,0:T(8,128)(2,1)} %copy-done.20) | copy-start | bytes 3538948
  229.2 10.2 %copy-start.37 = (bf16[384,1536]{1,0:T(8,128)(2,1)S(1)}, bf16[384,1536]{1,0:T(8,128)(2,1)}, u32[]{:S(2)}) copy-start(bf16[384,1536]{1,0:T(8,128)(2,1)} %copy-done.36) | copy-start | bytes 3538948
  229.2 29.2 %collective-permute-start.13 = (bf16[384,1536]{1,0:T(8,128)(2,1)}, bf16[384,1536]{1,0:T(8,128)(2,1)S(1)}, u32[]{:S(2)}, u32[]{:S(2)}) collective-permute-start(bf16[384,1536]{1,0:T(8,128)(2,1)} %copy-done.22), channel_id=1, source_target_pairs={{0,2},{2,0},{1,3},{3,1},{4,6},{6,4},{5,7},{7,5},{8,10},{10,8},{9,1... | collective-permute-start | bytes 3538952 | tf_op jit(solution)/shard_map/ppermute | solution.py:186
  238.1 20.3 %copy-start.23 = (bf16[384,1536]{1,0:T(8,128)(2,1)S(1)}, bf16[384,1536]{1,0:T(8,128)(2,1)}, u32[]{:S(2)}) copy-start(bf16[384,1536]{1,0:T(8,128)(2,1)} %copy-done.22) | copy-start | bytes 3538948
  238.1 41.1 %collective-permute-start.12 = (bf16[384,1536]{1,0:T(8,128)(2,1)S(1)}, bf16[384,1536]{1,0:T(8,128)(2,1)S(1)}, u32[]{:S(2)}, u32[]{:S(2)}) collective-permute-start(bf16[384,1536]{1,0:T(8,128)(2,1)S(1)} %shard_map.81.refs_0_), channel_id=1, source_target_pairs={{0,2},{2,0},{1,3},{3,1},{4,6},{6,4},{5,7},{7,5},{8,10},{10,8},{9,1... | collective-permute-start | bytes 3538952 | tf_op jit(solution)/shard_map/ppermute | solution.py:186
  295.9 1.0 copy-start.31
  295.9 1.9 copy-start.33
  295.9 15.9 %copy-start.35 = (bf16[128,2048]{1,0:T(8,128)(2,1)S(1)}, bf16[128,2048]{1,0:T(8,128)(2,1)}, u32[]{:S(2)}) copy-start(bf16[128,2048]{1,0:T(8,128)(2,1)} %copy-done.34) | copy-start | bytes 1572868
  295.9 16.7 %copy-start.6 = (f32[128,3072]{1,0:T(8,128)S(1)}, f32[128,3072]{1,0:T(8,128)}, u32[]{:S(2)}) copy-start(f32[128,3072]{1,0:T(8,128)} %copy-done.5) | copy-start | bytes 4718596
  296.9 15.9 %copy-start.14 = (bf16[128,2048]{1,0:T(8,128)(2,1)S(1)}, bf16[128,2048]{1,0:T(8,128)(2,1)}, u32[]{:S(2)}) copy-start(bf16[128,2048]{1,0:T(8,128)(2,1)} %copy-done.13) | copy-start | bytes 1572868
  296.9 15.9 %copy-start.26 = (bf16[128,2048]{1,0:T(8,128)(2,1)S(1)}, bf16[128,2048]{1,0:T(8,128)(2,1)}, u32[]{:S(2)}) copy-start(bf16[128,2048]{1,0:T(8,128)(2,1)} %copy-done.24) | copy-start | bytes 1572868
  296.9 14.9 %collective-permute-start.14 = (bf16[128,2048]{1,0:T(8,128)(2,1)S(1)}, bf16[128,2048]{1,0:T(8,128)(2,1)S(1)}, u32[]{:S(2)}, u32[]{:S(2)}) collective-permute-start(bf16[128,2048]{1,0:T(8,128)(2,1)S(1)} %copy-done.31), channel_id=1, source_target_pairs={{0,2},{2,0},{1,3},{3,1},{4,6},{6,4},{5,7},{7,5},{8,10},{10,8},{9,1... | collective-permute-start | bytes 1572872 | tf_op jit(solution)/shard_map/ppermute | solution.py:186
  297.8 25.3 %collective-permute-start.16 = (bf16[128,2048]{1,0:T(8,128)(2,1)S(1)}, bf16[128,2048]{1,0:T(8,128)(2,1)S(1)}, u32[]{:S(2)}, u32[]{:S(2)}) collective-permute-start(bf16[128,2048]{1,0:T(8,128)(2,1)S(1)} %copy-done.33), channel_id=1, source_target_pairs={{0,2},{2,0},{1,3},{3,1},{4,6},{6,4},{5,7},{7,5},{8,10},{10,8},{9,1... | collective-permute-start | bytes 1572872 | tf_op jit(solution)/shard_map/ppermute | solution.py:186
  311.8 18.1 %collective-permute-start.15 = (bf16[128,2048]{1,0:T(8,128)(2,1)S(1)}, bf16[128,2048]{1,0:T(8,128)(2,1)S(1)}, u32[]{:S(2)}, u32[]{:S(2)}) collective-permute-start(bf16[128,2048]{1,0:T(8,128)(2,1)S(1)} %copy-done.35), channel_id=1, source_target_pairs={{0,2},{2,0},{1,3},{3,1},{4,6},{6,4},{5,7},{7,5},{8,10},{10,8},{9,1... | collective-permute-start | bytes 1572872 | tf_op jit(solution)/shard_map/ppermute | solution.py:186
  312.7 7.1 %copy-start.38 = (bf16[128,3072]{1,0:T(8,128)(2,1)}, bf16[128,3072]{1,0:T(8,128)(2,1)S(1)}, u32[]{:S(2)}) copy-start(bf16[128,3072]{1,0:T(8,128)(2,1)S(1)} %convert_element_type.31) | copy-start | bytes 2359300
  312.8 10.3 %copy-start.12 = (bf16[128,2048]{1,0:T(8,128)(2,1)S(1)}, bf16[128,2048]{1,0:T(8,128)(2,1)}, u32[]{:S(2)}) copy-start(bf16[128,2048]{1,0:T(8,128)(2,1)} %copy-done.10) | copy-start | bytes 1572868
  312.8 24.1 %collective-permute-start.11 = (bf16[64,3072]{1,0:T(8,128)(2,1)S(1)}, bf16[64,3072]{1,0:T(8,128)(2,1)S(1)}, u32[]{:S(2)}, u32[]{:S(2)}) collective-permute-start(bf16[64,3072]{1,0:T(8,128)(2,1)S(1)} %slice.17), channel_id=1, source_target_pairs={{0,1},{1,0},{2,3},{3,2},{4,5},{5,4},{6,7},{7,6},{8,9},{9,8},{10,11... | collective-permute-start | bytes 1179656 | tf_op jit(solution)/shard_map/ppermute | solution.py:227
  319.9 10.1 %copy-start.9 = (bf16[128,2048]{1,0:T(8,128)(2,1)S(1)}, bf16[128,2048]{1,0:T(8,128)(2,1)}, u32[]{:S(2)}) copy-start(bf16[128,2048]{1,0:T(8,128)(2,1)} %copy-done.7) | copy-start | bytes 1572868
  319.9 10.1 %copy-start.29 = (bf16[128,2048]{1,0:T(8,128)(2,1)S(1)}, bf16[128,2048]{1,0:T(8,128)(2,1)}, u32[]{:S(2)}) copy-start(bf16[128,2048]{1,0:T(8,128)(2,1)} %copy-done.27) | copy-start | bytes 1572868
  336.7 1.1 copy-start.39
  336.8 2.9 collective-permute-start.17
Sparse Core Ops, SparseCore 0:
  9.6 40.9 all-gather.2
  52.3 37.1 all-gather.4
  229.3 40.9 reduce-scatter.2
  296.0 41.0 reduce-scatter.4
